TPU v7x, 32 devices: a whole 2x2x4 slice. The times are simulated.
32 devices in a mesh: ens: 2 (over y), tile: 4 (over z), chan: 2 (over x), sec: 2 (over core).
Axes of the slice: x: 2, y: 2, z: 4, core: 2. Of those that a mesh axis runs over, the one named last changes fastest.
Arguments:
- ocean_state: bfloat16 [256, 128, 4, 128], P(('chan', 'sec'), ('ens', 'tile')), parts along dimension 1, may hold values from -6 to 6
- atmos: bfloat16 [16384, 384], P(('ens', 'tile')), parts along dimension 0, may hold values from -6 to 6
- flux_weight: bfloat16 [384, 256], P(None, ('chan', 'sec')), may hold values from -0.3125 to 0.3125
- conv_weight: bfloat16 [9, 256, 256], P(None, None, ('chan', 'sec')), may hold values from -0.125 to 0.125
- conv_bias: bfloat16 [256], P(('chan', 'sec')), may hold values from -3 to 3
- norm_gain: bfloat16 [256], P(('chan', 'sec')), may hold values from 0.5 to 2
- in_weight: bfloat16 [256, 1024], P(None, ('chan', 'sec')), may hold values from -0.375 to 0.375
- in_bias: bfloat16 [1024], P(('chan', 'sec')), may hold values from -3 to 3
- out_weight: bfloat16 [1024, 256], P(('chan', 'sec')), may hold values from -0.25 to 0.25
- layer_scale: bfloat16 [256], P(('chan', 'sec')), may hold values from 0.5 to 2
- cell_mask: int32 [64, 4, 128], P('tile'), may hold values from 0 to 1, as said below
- neighbours: int32 [64, 8], P('tile'), may hold values from -1 to 63, as said below
- remap: int32 [64, 4, 128], P('tile'), may hold values from 0 to 8191
Outputs:
- ocean_next: bfloat16 [256, 128, 4, 128], P(('chan', 'sec'), ('ens', 'tile')), parts along dimension 1
There are 2 independent parts, one for each index of `ens`. A program takes and returns all parts, laid end to end along the dimension named above; an argument that names none is the same for every part. Nothing has to cross between parts.
Inputs may be any that keep to these rules, and one draw needn't show every extreme that they name: `cell_mask`: land cells and every cell of a land block are 0. `neighbours`: for a slot among those of tile index t, each entry is -1 or a slot among those of tile indices t - 1, t and t + 1, i.e. in [(t - 1) * 16, (t + 2) * 16); entries that name land blocks are -1.
All inputs are finite; a program needn't handle non-finite values.
Results may differ from a plain program's by a relative error of at most 0.01.
Values may be sent and summed in bfloat16 or wider, within the bound.
No kernel may reach another device: no remote copies, remote signals or barrier semaphores. Data moves between devices by JAX's collectives and lax.ppermute only.
A program may use at most 64 MiB of HBM per device.

v0:
```python
import jax
import jax.numpy as jnp
from jax import lax
from jax.sharding import PartitionSpec as P

norm_eps = 1e-06


def padded_2(cells, sides, width):
    for axis, dim in sides:
        count = lax.axis_size(axis)
        ends = count - 1
        head = lax.slice_in_dim(cells, 0, width, axis=dim)
        tail = lax.slice_in_dim(cells, cells.shape[dim] - width, cells.shape[dim], axis=dim)
        cells = jnp.concatenate(
            [
                lax.ppermute(tail, axis, [(i, (i + 1) % count) for i in range(ends)]),
                cells,
                lax.ppermute(head, axis, [((i + 1) % count, i) for i in range(ends)]),
            ],
            axis=dim,
        )
    return cells


def strips_of(state):
    return jnp.concatenate(
        [
            state[:, :, 0, :],
            state[:, :, -1, :],
            state[:, :, :, 0],
            state[:, :, :, -1],
            state[:, :, 0, 0:1],
            state[:, :, 0, -1:],
            state[:, :, -1, 0:1],
            state[:, :, -1, -1:],
        ],
        axis=2,
    )


def pad_blocks(state, strips, slot_index, valid):
    channels, slot_count, block_rows, block_cols = state.shape
    width = strips.shape[2]
    picked = jnp.take(strips, slot_index.reshape(-1), axis=1).reshape(
        channels, slot_count, 8, width
    )
    picked = jnp.where(valid[None, :, :, None], picked, jnp.zeros_like(picked))
    offset_base = 2 * block_cols + 2 * block_rows
    west_col = picked[:, :, 0, 2 * block_cols + block_rows : offset_base]
    east_col = picked[:, :, 1, 2 * block_cols : 2 * block_cols + block_rows]
    prev_row = picked[:, :, 2, block_cols : 2 * block_cols]
    next_row = picked[:, :, 3, 0:block_cols]
    top_row = jnp.concatenate(
        [
            picked[:, :, 4, offset_base + 3 : offset_base + 4],
            prev_row,
            picked[:, :, 5, offset_base + 2 : offset_base + 3],
        ],
        axis=2,
    )
    bottom_row = jnp.concatenate(
        [
            picked[:, :, 6, offset_base + 1 : offset_base + 2],
            next_row,
            picked[:, :, 7, offset_base : offset_base + 1],
        ],
        axis=2,
    )
    middle = jnp.concatenate([west_col[:, :, :, None], state, east_col[:, :, :, None]], axis=3)
    return jnp.concatenate([top_row[:, :, None, :], middle, bottom_row[:, :, None, :]], axis=2)


def conv_taps(padded, kernel, block_rows, block_cols):
    total = jnp.zeros((kernel.shape[2], padded.shape[1], block_rows, block_cols), jnp.float32)
    for tap in range(9):
        tap_row = tap // 3
        tap_col = tap % 3
        window = padded[:, :, tap_row : tap_row + block_rows, tap_col : tap_col + block_cols]
        total = total + jnp.einsum(
            "cskl,co->oskl", window, kernel[tap], preferred_element_type=jnp.float32
        )
    return total


def add_group(total, pair):
    term = jnp.einsum("hsij,hc->csij", pair[0], pair[1], preferred_element_type=jnp.float32).astype(
        jnp.bfloat16
    )
    term = lax.optimization_barrier(term)
    return (total + term.astype(jnp.float32), None)


def on_device(
    ocean_state,
    atmos,
    flux_weight,
    conv_weight,
    conv_bias,
    norm_gain,
    in_weight,
    in_bias,
    out_weight,
    layer_scale,
    cell_mask,
    neighbours,
    remap,
):
    chan_local, slot_count, block_rows, block_cols = ocean_state.shape
    groups = lax.axis_size(("chan", "sec"))
    channels = chan_local * groups
    hid_local = in_weight.shape[1]
    extended = padded_2(strips_of(ocean_state), (("tile", 1),), slot_count)
    first_slot = (lax.axis_index("tile") - 1) * slot_count
    valid = neighbours >= 0
    slot_index = jnp.clip(neighbours - first_slot, 0, 3 * slot_count - 1)
    padded = pad_blocks(ocean_state, extended, slot_index, valid)
    local_flux = jnp.einsum(
        "rf,fc->cr", atmos, flux_weight, preferred_element_type=jnp.float32
    ).astype(jnp.bfloat16)
    targets = remap.reshape(-1)
    piece = lax.all_gather(local_flux, "tile", axis=1, tiled=True)
    inside = (targets >= 0) & (targets < piece.shape[1])
    values = jnp.take(piece, jnp.clip(targets, 0, piece.shape[1] - 1), axis=1)
    forcing = jnp.where(inside[None, :], values, jnp.zeros_like(values))
    full_kernel, full_bias, full_gain, full_in, full_in_bias, full_out = (
        lax.all_gather(conv_weight, ("chan", "sec"), axis=2, tiled=True),
        lax.all_gather(conv_bias, ("chan", "sec"), axis=0, tiled=True),
        lax.all_gather(norm_gain, ("chan", "sec"), axis=0, tiled=True),
        lax.all_gather(in_weight, ("chan", "sec"), axis=1, tiled=True),
        lax.all_gather(in_bias, ("chan", "sec"), axis=0, tiled=True),
        lax.all_gather(out_weight, ("chan", "sec"), axis=0, tiled=True),
    )
    out_groups = full_out.reshape(groups, hid_local, channels)
    grouped = padded.reshape(
        chan_local, groups, slot_count // groups, block_rows + 2, block_cols + 2
    )
    tiles = lax.all_to_all(grouped, ("chan", "sec"), split_axis=1, concat_axis=0, tiled=True)[:, 0]
    conv_out = (
        conv_taps(tiles, full_kernel, block_rows, block_cols)
        + full_bias.astype(jnp.float32)[:, None, None, None]
    )
    squares = jnp.sum(conv_out * conv_out, axis=0)
    normed = (
        conv_out
        * lax.rsqrt(squares / channels + norm_eps)
        * full_gain.astype(jnp.float32)[:, None, None, None]
    ).astype(jnp.bfloat16)
    pre = jnp.einsum("csij,ch->hsij", normed, full_in, preferred_element_type=jnp.float32)
    hidden = jax.nn.gelu(
        pre + full_in_bias.astype(jnp.float32)[:, None, None, None], approximate=False
    ).astype(jnp.bfloat16)
    hid_groups = hidden.reshape((groups, hid_local) + hidden.shape[1:])
    summed, _ = lax.scan(
        add_group, jnp.zeros((channels,) + hidden.shape[1:], jnp.float32), (hid_groups, out_groups)
    )
    update = lax.all_to_all(
        summed[:, None], ("chan", "sec"), split_axis=0, concat_axis=1, tiled=True
    )
    update = update.reshape(chan_local, slot_count, block_rows, block_cols)
    total = (
        ocean_state.astype(jnp.float32)
        + layer_scale.astype(jnp.float32)[:, None, None, None] * update
    )
    total = total + forcing.reshape(chan_local, slot_count, block_rows, block_cols).astype(
        jnp.float32
    )
    return (cell_mask.astype(jnp.float32)[None] * total).astype(jnp.bfloat16)


def solution(mesh):
    placed = (
        P(("chan", "sec"), ("ens", "tile"), None, None),
        P(("ens", "tile"), None),
        P(None, ("chan", "sec")),
        P(None, None, ("chan", "sec")),
        P(("chan", "sec")),
        P(("chan", "sec")),
        P(None, ("chan", "sec")),
        P(("chan", "sec")),
        P(("chan", "sec"), None),
        P(("chan", "sec")),
        P("tile", None, None),
        P("tile", None),
        P("tile", None, None),
    )
    return jax.shard_map(
        on_device,
        mesh=mesh,
        in_specs=placed,
        out_specs=P(("chan", "sec"), ("ens", "tile"), None, None),
        check_vma=False,
    )
```

profile of v0, /device:TPU:0, one launch (start us, length us, event | category | flops | bytes accessed | tf_op | source)
XLA Modules:
  0.0 303.2 jit_solution(8548367868448448992)
XLA Ops:
  6.5 3.6 %fusion.51 = (bf16[64,16,1,128]{3,2,1,0:T(2,128)(2,1)S(1)}, bf16[64,16,1,128]{3,2,1,0:T(2,128)(2,1)}) fusion(bf16[64,16,4,128]{3,2,1,0:T(4,128)(2,1)} %param.15), kind=kLoop, calls=%fused_computation.95 | loop fusion | bytes 1048576 | tf_op jit(solution)/shard_map/slice | solution.py:30
  10.2 3.0 fusion.49
  13.2 2.3 fusion.50
  15.5 1.3 copy.122
  16.8 0.9 copy.73
  17.7 1.3 copy.123
  19.0 0.9 copy.74
  19.9 1.3 copy.124
  21.2 0.9 copy.75
  22.1 1.3 copy.125
  23.4 0.9 copy.76
  24.3 7.2 %copy.136 = bf16[64,16,4,1]{2,0,1,3:T(8,128)(2,1)S(1)} copy(bf16[64,16,4,1]{3,2,1,0:T(4,128)(2,1)} %get-tuple-element.80) | data formatting | bytes 16384 | tf_op jit(solution)/shard_map/squeeze | solution.py:31
  31.6 7.9 %copy.137 = bf16[64,16,4,1]{2,0,1,3:T(8,128)(2,1)} copy(bf16[64,16,4,1]{3,2,1,0:T(4,128)(2,1)} %get-tuple-element.79) | data formatting | bytes 16384 | tf_op jit(solution)/shard_map/squeeze | solution.py:32
  39.5 2.2 copy_bitcast_fusion.1
  41.6 3.6 %concatenate.40 = bf16[64,16,268]{2,0,1:T(8,128)(2,1)} concatenate(bf16[64,16,128]{2,0,1:T(8,128)(2,1)} %get-tuple-element.89, bf16[64,16,128]{2,0,1:T(8,128)(2,1)} %get-tuple-element.88, bf16[64,16,4]{2,0,1:T(8,128)(2,1)S(1)} %bitcast.225, bf16[64,16,4]{2,0,1:T(8,128)(2,1)} %bitcast.226, bf16[64,16,1]{2,0,1:T(8,128)(2,1)} %copy.73, bf16[64,16,1]{2,0,1:T(8,128)(2,1)} %copy.74, ...), dimensions={2} | concatenate | bytes 1097728 | tf_op jit(solution)/shard_map/concatenate | solution.py:27
  45.3 5.8 %collective-permute-start = (bf16[64,16,268]{2,0,1:T(8,128)(2,1)}, bf16[64,16,268]{2,0,1:T(8,128)(2,1)}, u32[]{:S(2)}, u32[]{:S(2)}) collective-permute-start(bf16[64,16,268]{2,0,1:T(8,128)(2,1)} %concatenate.40), channel_id=1, source_target_pairs={{0,4},{4,8},{8,12},{1,5},{5,9},{9,13},{2,6},{6,10},{10,14},{3,7},{... | collective-permute-start | bytes 1646600 | tf_op jit(solution)/shard_map/ppermute | solution.py:17
  51.1 1.5 collective-permute-start.1
  52.6 1.6 copy.82
  54.4 12.9 %collective-permute-done = bf16[64,16,268]{2,0,1:T(8,128)(2,1)} collective-permute-done((bf16[64,16,268]{2,0,1:T(8,128)(2,1)}, bf16[64,16,268]{2,0,1:T(8,128)(2,1)}, u32[]{:S(2)}, u32[]{:S(2)}) %collective-permute-start) | collective-permute-done | bytes 548896 | tf_op jit(solution)/shard_map/ppermute | solution.py:17
  67.3 5.0 %collective-permute-done.1 = bf16[64,16,268]{2,0,1:T(8,128)(2,1)} collective-permute-done((bf16[64,16,268]{2,0,1:T(8,128)(2,1)}, bf16[64,16,268]{2,0,1:T(8,128)(2,1)}, u32[]{:S(2)}, u32[]{:S(2)}) %collective-permute-start.1) | collective-permute-done | bytes 548896 | tf_op jit(solution)/shard_map/ppermute | solution.py:19
  72.3 3.5 %pad_maximum_fusion.1 = bf16[64,48,268]{2,0,1:T(8,128)(2,1)} fusion(bf16[64,16,268]{2,0,1:T(8,128)(2,1)} %collective-permute-done.1, bf16[64,16,268]{2,0,1:T(8,128)(2,1)} %concatenate.40, bf16[64,16,268]{2,0,1:T(8,128)(2,1)} %collective-permute-done), kind=kLoop, calls=%fused_computation.35 | loop fusion | flops 1646592 | bytes 3293184 | tf_op jit(solution)/shard_map/concatenate | solution.py:15
  75.8 5.8 %gather_fusion = bf16[128,64,268]{2,1,0:T(8,128)(2,1)} fusion(bf16[64,48,268]{2,0,1:T(8,128)(2,1)} %pad_maximum_fusion.1, s32[1024]{0:T(1024)S(1)} %pad_clamp_fusion), kind=kCustom, calls=%fused_computation | custom fusion | bytes 8782336 | tf_op jit(solution)/shard_map/jit(_take)/gather | solution.py:45
  81.5 13.8 %copy.78 = bf16[64,16,8,268]{0,1,3,2:T(8,128)(2,1)} copy(bf16[64,16,8,268]{3,0,2,1:T(8,128)(2,1)} %bitcast.217) | data formatting | bytes 8781824 | tf_op jit(solution)/shard_map/jit(_take)/gather | solution.py:45
  95.3 7.9 %select_select_fusion = bf16[64,16,8,268]{0,1,3,2:T(8,128)(2,1)} fusion(bf16[64,16,8,268]{0,1,3,2:T(8,128)(2,1)} %copy.78, pred[16,8]{0,1:T(8,128)(4,1)S(1)} %get-tuple-element.65, pred[16,8]{0,1:T(8,128)(4,1)S(1)} %get-tuple-element.85), kind=kLoop, calls=%fused_computation.10 | loop fusion | flops 4390912 | bytes 8782080 | tf_op jit(solution)/shard_map/jit(_where)/select_n | solution.py:48
  103.2 0.7 fusion.46
  103.9 0.9 copy.80
  104.9 0.9 copy.81
  105.8 1.4 fusion.47
  107.6 0.9 copy.86
  108.5 0.9 copy.87
  109.4 1.2 copy.85
  110.6 0.7 fusion.48
  111.3 1.5 copy.83
  112.8 1.4 copy.84
  114.2 1.5 maximum_bitcast_fusion
  115.7 1.4 maximum_bitcast_fusion.1
  117.2 3.0 pad_maximum_fusion
  120.3 4.8 %all-to-all-start = ((bf16[64,4,4,6,130]{4,0,3,2,1:T(8,128)(2,1)}), bf16[64,4,4,6,130]{4,0,3,2,1:T(8,128)(2,1)}, u32[]{:S(2)}, u32[]{:S(2)}) async-start(bf16[64,4,4,6,130]{4,0,3,2,1:T(8,128)(2,1)} %pad_maximum_fusion), calls=%async_computation | async-start | bytes 6291456 | tf_op jit(solution)/shard_map/all_to_all | solution.py:138
  125.1 1.3 convolution_convert_fusion.1
  128.3 35.2 %all-reduce.2 = (bf16[256]{0:T(256)(128)(2,1)S(1)}, bf16[256]{0:T(256)(128)(2,1)S(1)}) all-reduce(bf16[256]{0:T(256)(128)(2,1)S(1)} %dynamic-update-slice, bf16[256]{0:T(256)(128)(2,1)S(1)} %dynamic-update-slice.1), channel_id=1, replica_groups=mesh['ens'=2,'tile'=4,'chan'=2,'sec'=2] {'chan','sec'}, use_global_device_ids=true, to_apply=%add | all-reduce | flops 512 | bytes 2048
  163.5 5.1 %all-gather = bf16[4,1,256]{2,1,0:T(2,128)(2,1)S(1)} all-gather(bf16[1,1,256]{2,1,0:T(2,128)(2,1)S(1)} %reshape.159), channel_id=1, replica_groups=mesh['ens'=2,'tile'=4,'chan'=2,'sec'=2] {'chan','sec'}, dimensions={0}, use_global_device_ids=true | all-gather | bytes 2560 | tf_op jit(solution)/shard_map/all_gather | solution.py:131
  168.6 7.3 %all_gather.25 = bf16[256,1024]{1,0:T(8,128)(2,1)S(1)} all-gather(bf16[256,256]{1,0:T(8,128)(2,1)S(1)} %copy-done.10), channel_id=1, replica_groups=mesh['ens'=2,'tile'=4,'chan'=2,'sec'=2] {'chan','sec'}, dimensions={1}, use_global_device_ids=true | all-gather | bytes 655360 | tf_op jit(solution)/shard_map/all_gather | solution.py:130
  176.0 7.9 %all_gather.21 = bf16[1024,256]{1,0:T(8,128)(2,1)} all-gather(bf16[256,256]{1,0:T(8,128)(2,1)S(1)} %copy-done.11), channel_id=1, replica_groups=mesh['ens'=2,'tile'=4,'chan'=2,'sec'=2] {'chan','sec'}, dimensions={0}, use_global_device_ids=true | all-gather | bytes 655360 | tf_op jit(solution)/shard_map/all_gather | solution.py:132
  184.0 7.3 %copy.90 = bf16[4,64,1,4,6,130]{1,0,5,4,3,2:T(4,128)(2,1)} copy(bf16[4,64,1,4,6,130]{5,1,4,3,0,2:T(8,128)(2,1)} %bitcast.24) | data formatting | bytes 3194880 | tf_op jit(solution)/shard_map/all_to_all | solution.py:138
  191.3 5.1 %squeeze.76 = bf16[256,4,6,130]{0,3,2,1:T(8,128)(2,1)} reshape(bf16[4,64,1,4,6,130]{1,0,5,4,3,2:T(4,128)(2,1)} %copy.90) | data formatting | bytes 3194880 | tf_op jit(solution)/shard_map/squeeze | solution.py:138
  196.4 1.8 fusion.28
  201.9 1.3 multiply_reduce_fusion
  203.1 20.7 %fusion.7 = bf16[1024,4,4,128]{0,3,2,1:T(8,128)(2,1)} fusion(f32[1024]{0:T(1024)S(1)} %bitcast.239, f32[4,4,128,256]{3,2,1,0:T(8,128)S(1)} %get-tuple-element.87, f32[256]{0:T(256)S(1)} %convert_element_type.43, f32[4,4,128]{2,1,0:T(4,128)S(1)} %add_rsqrt_fusion, bf16[256,1024]{1,0:T(8,128)(2,1)S(1)} %all_gather.25), kind=kOutput, calls=%fused_computation.13 | convolution fusion | flops 1213726720 | bytes 6829056 | tf_op jit(solution)/shard_map/csij,ch->hsij/dot_general | solution.py:149
  223.9 7.9 %reshape.135 = bf16[4,256,4,4,128]{1,0,4,3,2:T(4,128)(2,1)} reshape(bf16[1024,4,4,128]{0,3,2,1:T(8,128)(2,1)} %fusion.7) | data formatting | bytes 8388608 | tf_op jit(solution)/shard_map/reshape | solution.py:153
  231.8 7.5 %copy.101 = bf16[4,256,4,4,128]{4,1,3,2,0:T(8,128)(2,1)} copy(bf16[4,256,4,4,128]{1,0,4,3,2:T(4,128)(2,1)} %reshape.135) | data formatting | bytes 8388608
  239.3 9.9 %while.11 = (s32[]{:T(128)}, f32[256,4,4,128]{3,0,2,1:T(8,128)S(1)}, bf16[4,256,256]{2,1,0:T(8,128)(2,1)}, bf16[4,256,4,4,128]{4,1,3,2,0:T(8,128)(2,1)}, s32[]{:T(128)}, /*index=5*/s32[]{:T(128)}) while((s32[]{:T(128)}, f32[256,4,4,128]{3,0,2,1:T(8,128)S(1)}, bf16[4,256,256]{2,1,0:T(8,128)(2,1)}, ...), condition=%wide.region_2.3_spmd.clone, body=%wide.region_1.2_spmd.clone.sunk | while | flops 270532608 | bytes 7472207 | solution.py:154
  239.3 1.8 convolution_convert_fusion.3
  241.0 0.7 select_add_fusion.2
  241.7 1.8 convolution_convert_fusion.3
  244.2 1.8 convolution_convert_fusion.3
  246.0 0.7 select_add_fusion.2
  246.7 1.8 convolution_convert_fusion.3
  249.2 2.7 copy.141
  251.8 4.7 %all-to-all-start.1 = ((f32[256,1,4,4,128]{4,3,2,1,0:T(4,128)}), f32[256,1,4,4,128]{4,3,2,1,0:T(4,128)}, u32[]{:S(2)}, u32[]{:S(2)}) async-start(f32[256,1,4,4,128]{4,3,2,1,0:T(4,128)} %bitcast.218), calls=%async_computation.1 | async-start | bytes 4194304 | tf_op jit(solution)/shard_map/all_to_all | solution.py:157
  256.6 2.0 copy.104
  258.7 29.2 %gather_fusion.1 = bf16[8192,64]{1,0:T(8,128)(2,1)} fusion(bf16[64,8192]{0,1:T(8,128)(2,1)S(1)} %copy.104, s32[8192]{0:T(1024)S(1)} %broadcast_clamp_fusion), kind=kCustom, calls=%fused_computation.1 | custom fusion | bytes 2129920 | tf_op jit(solution)/shard_map/jit(_take)/gather | solution.py:124
  287.9 3.7 %copy.105 = bf16[64,16,4,128]{3,2,1,0:T(4,128)(2,1)} copy(bf16[64,16,4,128]{0,3,2,1:T(8,128)(2,1)} %bitcast.220) | data formatting | bytes 2097152 | tf_op jit(solution)/shard_map/jit(_take)/gather | solution.py:124
  291.6 2.3 copy.103
  294.0 2.4 multiply_convert_fusion.1
  (82 shorter events, 7.1 us)
Async XLA Ops:
  6.5 118.6 %copy-start = (bf16[2048,384]{1,0:T(8,128)(2,1)S(1)}, bf16[2048,384]{1,0:T(8,128)(2,1)}, u32[]{:S(2)}) copy-start(bf16[2048,384]{1,0:T(8,128)(2,1)} %param.16) | copy-start | bytes 4718596
  6.5 3.6 %copy-start.3 = (bf16[64,16,4,128]{3,2,1,0:T(4,128)(2,1)S(1)}, bf16[64,16,4,128]{3,2,1,0:T(4,128)(2,1)}, u32[]{:S(2)}) copy-start(bf16[64,16,4,128]{3,2,1,0:T(4,128)(2,1)} %param.15) | copy-start | bytes 3145732
  6.5 189.8 %all-gather.4.cloned.1.call-start = ((), (), s32[]{:S(2)}) async-start(), calls=%async_computation.2 | async-start | bytes 1474560 | tf_op jit(solution)/shard_map/all_gather | solution.py:127
  39.5 14.8 %copy-start.15 = (s32[16,8]{0,1:T(8,128)S(1)}, s32[16,8]{0,1:T(8,128)}, u32[]{:S(2)}) copy-start(s32[16,8]{0,1:T(8,128)} %param.26) | copy-start | bytes 1540
  45.3 22.0 %collective-permute-start = (bf16[64,16,268]{2,0,1:T(8,128)(2,1)}, bf16[64,16,268]{2,0,1:T(8,128)(2,1)}, u32[]{:S(2)}, u32[]{:S(2)}) collective-permute-start(bf16[64,16,268]{2,0,1:T(8,128)(2,1)} %concatenate.40), channel_id=1, source_target_pairs={{0,4},{4,8},{8,12},{1,5},{5,9},{9,13},{2,6},{6,10},{10,14},{3,7},{... | collective-permute-start | bytes 1646600 | tf_op jit(solution)/shard_map/ppermute | solution.py:17
  51.1 21.2 %collective-permute-start.1 = (bf16[64,16,268]{2,0,1:T(8,128)(2,1)}, bf16[64,16,268]{2,0,1:T(8,128)(2,1)}, u32[]{:S(2)}, u32[]{:S(2)}) collective-permute-start(bf16[64,16,268]{2,0,1:T(8,128)(2,1)} %concatenate.40), channel_id=1, source_target_pairs={{4,0},{8,4},{12,8},{5,1},{9,5},{13,9},{6,2},{10,6},{14,10},{7,3},{... | collective-permute-start | bytes 1646600 | tf_op jit(solution)/shard_map/ppermute | solution.py:19
  107.6 9.6 %copy-start.5 = (bf16[64,16,4,128]{3,0,2,1:T(8,128)(2,1)S(1)}, bf16[64,16,4,128]{3,0,2,1:T(8,128)(2,1)}, u32[]{:S(2)}) copy-start(bf16[64,16,4,128]{3,0,2,1:T(8,128)(2,1)} %copy.82) | copy-start | bytes 3145732
  114.2 2.9 copy-start.6
  114.2 2.9 copy-start.7
  120.2 4.9 %copy-start.13 = (bf16[384,64]{0,1:T(8,128)(2,1)S(1)}, bf16[384,64]{0,1:T(8,128)(2,1)}, u32[]{:S(2)}) copy-start(bf16[384,64]{0,1:T(8,128)(2,1)} %param.17) | copy-start | bytes 147460
  120.2 6.3 %copy-start.20 = (u32[32]{0:T(128)S(1)}, u32[32]{0:T(128)}, u32[]{:S(2)}) copy-start(u32[32]{0:T(128)} %constant.127) | copy-start | bytes 388
  120.2 7.6 %copy-start.16 = (bf16[64]{0:T(256)(128)(2,1)S(1)}, bf16[64]{0:T(256)(128)(2,1)}, u32[]{:S(2)}) copy-start(bf16[64]{0:T(256)(128)(2,1)} %param.19) | copy-start | bytes 388
  120.2 7.8 %copy-start.17 = (bf16[64]{0:T(256)(128)(2,1)S(1)}, bf16[64]{0:T(256)(128)(2,1)}, u32[]{:S(2)}) copy-start(bf16[64]{0:T(256)(128)(2,1)} %param.20) | copy-start | bytes 388
  120.2 43.3 %copy-start.18 = (bf16[256]{0:T(256)(128)(2,1)S(1)}, bf16[256]{0:T(256)(128)(2,1)}, u32[]{:S(2)}) copy-start(bf16[256]{0:T(256)(128)(2,1)} %param.22) | copy-start | bytes 1540
  120.2 48.4 %copy-start.14 = (s32[16,4,128]{2,1,0:T(4,128)S(1)}, s32[16,4,128]{2,1,0:T(4,128)}, u32[]{:S(2)}) copy-start(s32[16,4,128]{2,1,0:T(4,128)} %param.25) | copy-start | bytes 98308
  120.2 48.4 %copy-start.19 = (bf16[64]{0:T(256)(128)(2,1)S(1)}, bf16[64]{0:T(256)(128)(2,1)}, u32[]{:S(2)}) copy-start(bf16[64]{0:T(256)(128)(2,1)} %param.24) | copy-start | bytes 388
  120.3 48.4 %copy-start.10 = (bf16[256,256]{1,0:T(8,128)(2,1)S(1)}, bf16[256,256]{1,0:T(8,128)(2,1)}, u32[]{:S(2)}) copy-start(bf16[256,256]{1,0:T(8,128)(2,1)} %param.21) | copy-start | bytes 393220
  120.3 55.7 %copy-start.11 = (bf16[256,256]{1,0:T(8,128)(2,1)S(1)}, bf16[256,256]{1,0:T(8,128)(2,1)}, u32[]{:S(2)}) copy-start(bf16[256,256]{1,0:T(8,128)(2,1)} %param.23) | copy-start | bytes 393220
  120.3 63.7 %all-to-all-start = ((bf16[64,4,4,6,130]{4,0,3,2,1:T(8,128)(2,1)}), bf16[64,4,4,6,130]{4,0,3,2,1:T(8,128)(2,1)}, u32[]{:S(2)}, u32[]{:S(2)}) async-start(bf16[64,4,4,6,130]{4,0,3,2,1:T(8,128)(2,1)} %pad_maximum_fusion), calls=%async_computation | async-start | bytes 6291456 | tf_op jit(solution)/shard_map/all_to_all | solution.py:138
  125.1 58.9 %copy-start.12 = (s32[16,4,128]{2,1,0:T(4,128)S(1)}, s32[16,4,128]{2,1,0:T(4,128)}, u32[]{:S(2)}) copy-start(s32[16,4,128]{2,1,0:T(4,128)} %param.27) | copy-start | bytes 98308
  125.1 131.5 %all-gather.6.cloned.1.call-start = ((), (), s32[]{:S(2)}) async-start(), calls=%async_computation.3 | async-start | bytes 1310720 | tf_op jit(solution)/shard_map/all_gather | solution.py:122
  196.4 1.9 copy-start.2
  196.4 2.1 copy-start.9
  251.8 39.8 %all-to-all-start.1 = ((f32[256,1,4,4,128]{4,3,2,1,0:T(4,128)}), f32[256,1,4,4,128]{4,3,2,1,0:T(4,128)}, u32[]{:S(2)}, u32[]{:S(2)}) async-start(f32[256,1,4,4,128]{4,3,2,1,0:T(4,128)} %bitcast.218), calls=%async_computation.1 | async-start | bytes 4194304 | tf_op jit(solution)/shard_map/all_to_all | solution.py:157
  287.9 6.1 %copy-start.4 = (bf16[64,16,4,128]{3,2,1,0:T(4,128)(2,1)S(1)}, bf16[64,16,4,128]{3,2,1,0:T(4,128)(2,1)}, u32[]{:S(2)}) copy-start(bf16[64,16,4,128]{3,2,1,0:T(4,128)(2,1)} %param.15) | copy-start | bytes 3145732
  291.6 2.3 copy-start.8
  291.6 4.7 %copy-start.1 = (bf16[2048,384]{1,0:T(8,128)(2,1)S(1)}, bf16[2048,384]{1,0:T(8,128)(2,1)}, u32[]{:S(2)}) copy-start(bf16[2048,384]{1,0:T(8,128)(2,1)} %param.16) | copy-start | bytes 4718596
Sparse Core Ops, SparseCore 0:
  52.7 19.5 all-gather.3
  127.5 27.7 all-gather.5
where the time goes:
time: 305 us; the launch traced here: 303 us
  local copies, waits for them, and re-layouts  140 us (46%)
  blocking collectives  55.6 us (18%)
  matrix products  35.6 us (12%)
  other arithmetic  22.6 us (7%)
  waiting for transfers between devices  17.9 us (6%)
  starting transfers between devices  16.8 us (6%)
  between operations  14.4 us (5%)
    unnamed x1, blocking collectives  35.2 us
    gather x2, local copies, waits for them, and re-layouts, on_device(): values = jnp.take(piece, jnp.clip(targets, 0, piece.shape[1] - 1), axis=1)  32.9 us
    dot_general x1, matrix products, on_device(): jnp.einsum('csij,ch->hsij', normed, full_in, preferred_element_type=jnp.f...  20.7 us
    gather x2, local copies, waits for them, and re-layouts, pad_blocks(): jnp.take(strips, slot_index.reshape(-1), axis=1)  19.6 us
    unnamed x54, local copies, waits for them, and re-layouts  15.9 us
    ppermute x1, waiting for transfers between devices, padded_2(): lax.ppermute(tail, axis, [(i, (i + 1) % count) for i in range(ends)])  12.9 us
    all_gather x1, blocking collectives, on_device(): lax.all_gather(out_weight, ('chan', 'sec'), axis=0, tiled=True)  7.95 us
    select_n x1, other arithmetic, pad_blocks(): picked = jnp.where(valid[None, :, :, None], picked, jnp.zeros_like(picked))  7.94 us
  transfers between devices with their start and end apart: 6, of which 2 were waited for; matrix products, arithmetic and copies ran while one was open for 51% of the time, Pallas kernels for 0%

commit v1 on v0

v1 whole, which is shorter than its diff:
```python
import functools

import jax
import jax.numpy as jnp
from jax import lax
from jax.experimental import pallas as pl
from jax.experimental.pallas import tpu as pltpu
from jax.sharding import PartitionSpec as P

norm_eps = 1e-06
bf16 = jnp.bfloat16
f32 = jnp.float32
GROUP = ("chan", "sec")
BIAS_ROWS = 32
VMEM = pl.BlockSpec(memory_space=pltpu.VMEM)
SMEM = pl.BlockSpec(memory_space=pltpu.SMEM)


def shape(dims, dtype=bf16):
    return jax.ShapeDtypeStruct(dims, dtype)


def params(mib=48):
    return pltpu.CompilerParams(vmem_limit_bytes=mib * 1024 * 1024)


def ein(a, b, dims):
    return lax.dot_general(a, b, (dims, ((), ())), preferred_element_type=f32)


def prep_kernel(state_ref, xt_ref, strips_ref):
    chan_local, slot_count, block_rows, block_cols = state_ref.shape
    lane = lax.broadcasted_iota(jnp.int32, (chan_local, block_cols), 1)
    cols = jnp.zeros((chan_local, block_cols), f32)
    for s in range(slot_count):
        rows = jnp.swapaxes(state_ref[:, s].astype(f32), 0, 1)
        packed = rows.astype(bf16)
        xt_ref[s] = packed
        strips_ref[2 * s] = packed[0]
        strips_ref[2 * s + 1] = packed[block_rows - 1]
        for r in range(block_rows):
            at = 2 * (block_rows * s + r)
            turned = pltpu.roll(rows[r], at + 1, 1)
            cols = jnp.where((lane == at) | (lane == at + 1), turned, cols)
    strips_ref[2 * slot_count] = cols.astype(bf16)


def prep(state):
    chan_local, slot_count, block_rows, block_cols = state.shape
    return pl.pallas_call(
        prep_kernel,
        out_shape=(
            shape((slot_count, block_rows, chan_local, block_cols)),
            shape((2 * slot_count + 1, chan_local, block_cols)),
        ),
        in_specs=[VMEM],
        out_specs=(VMEM, VMEM),
        compiler_params=params(),
        name="prep_state",
    )(state)


def pack_kernel(conv_ref, bias_ref, gain_ref, in_ref, in_bias_ref, out_ref, pack_ref):
    taps, chan_local, channels = conv_ref.shape
    hid_local = out_ref.shape[0]
    for t in range(taps):
        pack_ref[pl.ds(t * chan_local, chan_local), :] = conv_ref[t]
    at = taps * chan_local
    pack_ref[pl.ds(at, hid_local), :] = in_ref[...].astype(f32).T.astype(bf16)
    pack_ref[pl.ds(at + hid_local, hid_local), :] = out_ref[...]

    def widen(row):
        row = row.astype(f32)
        if row.shape[1] == channels:
            return row
        return jnp.concatenate([row, jnp.zeros((1, channels - row.shape[1]), f32)], axis=1)

    rest = jnp.zeros((BIAS_ROWS - 3, channels), f32)
    biases = jnp.concatenate(
        [widen(bias_ref[...]), widen(gain_ref[...]), widen(in_bias_ref[...]), rest], axis=0
    )
    pack_ref[pl.ds(at + 2 * hid_local, BIAS_ROWS), :] = biases.astype(bf16)


def pack_weights(conv_weight, conv_bias, norm_gain, in_weight, in_bias, out_weight):
    taps, channels, chan_local = conv_weight.shape
    hid_local = out_weight.shape[0]
    return pl.pallas_call(
        pack_kernel,
        out_shape=shape((taps * chan_local + 2 * hid_local + BIAS_ROWS, channels)),
        in_specs=[VMEM] * 6,
        out_specs=VMEM,
        compiler_params=params(),
        name="pack_weights",
    )(
        conv_weight.transpose(0, 2, 1),
        conv_bias[None],
        norm_gain[None],
        in_weight,
        in_bias[None],
        out_weight,
    )


def unpack_kernel(chan_local, hid_local, all_ref, conv_ref, in_ref, out_ref, col_ref, hid_col_ref):
    groups, _, channels = all_ref.shape
    at = 9 * chan_local
    rows = []
    for j in range(groups):
        for t in range(9):
            conv_ref[pl.ds(j * chan_local, chan_local), pl.ds(t * channels, channels)] = all_ref[
                j, pl.ds(t * chan_local, chan_local), :
            ]
        in_ref[pl.ds(j * hid_local, hid_local), :] = all_ref[j, pl.ds(at, hid_local), :]
        biases = all_ref[j, pl.ds(at + 2 * hid_local, BIAS_ROWS), :].astype(f32)
        across = biases.T
        col_ref[pl.ds(j * chan_local, chan_local), :] = across[:chan_local]
        hid_col_ref[pl.ds(j * hid_local, hid_local), :] = across[:hid_local]
    outs = jnp.concatenate(
        [all_ref[j, pl.ds(at + hid_local, hid_local), :] for j in range(groups)], axis=0
    )
    out_ref[...] = outs.astype(f32).T.astype(bf16)


def unpack_weights(gathered, chan_local, hid_local):
    groups, _, channels = gathered.shape
    hidden = groups * hid_local
    return pl.pallas_call(
        functools.partial(unpack_kernel, chan_local, hid_local),
        out_shape=(
            shape((channels, 9 * channels)),
            shape((hidden, channels)),
            shape((channels, hidden)),
            shape((channels, BIAS_ROWS), f32),
            shape((hidden, BIAS_ROWS), f32),
        ),
        in_specs=[VMEM],
        out_specs=(VMEM,) * 5,
        compiler_params=params(),
        name="unpack_weights",
    )(gathered)


def flux_kernel(atmos_ref, weight_ref, out_ref):
    rows, lanes = out_ref.shape
    chan_local, features = weight_ref.shape
    weight = weight_ref[...]
    total = jnp.zeros((rows, lanes), f32)
    for k in range(lanes // chan_local):
        parts = [weight if j == k else jnp.zeros_like(weight) for j in range(lanes // chan_local)]
        wide = jnp.concatenate(parts, axis=0)
        total = total + ein(atmos_ref[pl.ds(k * rows, rows), :], wide, ((1,), (1,)))
    out_ref[...] = total.astype(bf16)


def fluxes_of(atmos, flux_weight):
    side = 128 // flux_weight.shape[1]
    return pl.pallas_call(
        flux_kernel,
        out_shape=shape((atmos.shape[0] // side, 128)),
        in_specs=[VMEM, VMEM],
        out_specs=VMEM,
        compiler_params=params(),
        name="fluxes",
    )(atmos, flux_weight.T)


def rim_kernel(entry_ref, at_ref, prev_ref, own_ref, next_ref, rim_ref, held):
    tiles, chan_local, block_cols = own_ref.shape
    groups = rim_ref.shape[0]
    slot_count = (tiles - 1) // 2
    per = slot_count // groups
    held[pl.ds(0, tiles)] = prev_ref[...]
    held[pl.ds(tiles, tiles)] = own_ref[...]
    held[pl.ds(2 * tiles, tiles)] = next_ref[...]
    held[3 * tiles] = jnp.zeros((chan_local, block_cols), bf16)
    ends = jnp.concatenate(
        [prev_ref[tiles - 1], own_ref[tiles - 1], next_ref[tiles - 1]], axis=1
    )
    spot = lax.broadcasted_iota(jnp.int32, (3 * block_cols, block_cols), 0)
    for d in range(groups):
        for s in range(per):
            rim_ref[d, 2 * s] = held[entry_ref[0, d * per + s]]
            rim_ref[d, 2 * s + 1] = held[entry_ref[1, d * per + s]]
        chosen = (spot == at_ref[pl.ds(d, 1), :]).astype(f32).astype(bf16)
        rim_ref[d, 2 * per] = ein(ends, chosen, ((1,), (0,))).astype(bf16)


def rims_of(strips_prev, strips, strips_next, neighbours, first_slot, groups):
    tiles, chan_local, block_cols = strips.shape
    slot_count = (tiles - 1) // 2
    per = slot_count // groups
    block_rows = block_cols // (2 * slot_count)
    valid = neighbours >= 0
    slot = jnp.clip(neighbours - first_slot, 0, 3 * slot_count - 1)
    tile_of = slot // slot_count
    place = tile_of * tiles + 2 * (slot - tile_of * slot_count)
    entries = jnp.stack(
        [
            jnp.where(valid[:, 2], place[:, 2] + 1, 3 * tiles),
            jnp.where(valid[:, 3], place[:, 3], 3 * tiles),
        ]
    )
    base = jnp.where(valid, 2 * block_rows * slot, -2 * block_rows * 2)
    last = 2 * (block_rows - 1)
    west = [base[:, 4] + last] + [base[:, 0] + 2 * r for r in range(block_rows)] + [base[:, 6]]
    east = [base[:, 5] + last] + [base[:, 1] + 2 * r for r in range(block_rows)] + [base[:, 7]]
    none = [jnp.full((slot_count,), -1, jnp.int32)] * (8 - block_rows - 2)
    at = jnp.stack(west + none + [e + 1 for e in east] + none, axis=1)
    at = at.reshape(groups, per * 16)
    at = jnp.pad(at, ((0, 0), (0, block_cols - per * 16)), constant_values=-1)
    return pl.pallas_call(
        rim_kernel,
        out_shape=shape((groups, 2 * per + 1, chan_local, block_cols)),
        in_specs=[SMEM, VMEM, VMEM, VMEM, VMEM],
        out_specs=VMEM,
        scratch_shapes=[pltpu.VMEM((3 * tiles + 1, chan_local, block_cols), bf16)],
        compiler_params=params(),
        name="rims",
    )(entries, at, strips_prev, strips, strips_next)


def block_kernel(
    body_ref, rim_ref, conv_ref, in_ref, out_ref, col_ref, hid_col_ref, upd_ref, taken, hid
):
    groups, per, block_rows, chan_local, block_cols = body_ref.shape
    channels = groups * chan_local
    hidden = in_ref.shape[0]
    lane = lax.broadcasted_iota(jnp.int32, (chan_local, block_cols), 1)
    bias = col_ref[:, 0:1]
    gain = col_ref[:, 1:2]
    for s in range(per):
        for j in range(groups):
            ends = rim_ref[j, 2 * per].astype(f32)
            for p in range(block_rows + 2):
                if p == 0:
                    mid = rim_ref[j, 2 * s]
                elif p == block_rows + 1:
                    mid = rim_ref[j, 2 * s + 1]
                else:
                    mid = body_ref[j, s, p - 1]
                wide = mid.astype(f32)
                spot = 16 * s + p
                left = jnp.where(
                    lane == 0,
                    pltpu.roll(ends, (block_cols - spot) % block_cols, 1),
                    pltpu.roll(wide, 1, 1),
                ).astype(bf16)
                right = jnp.where(
                    lane == block_cols - 1,
                    pltpu.roll(ends, (2 * block_cols - 1 - spot - 8) % block_cols, 1),
                    pltpu.roll(wide, block_cols - 1, 1),
                ).astype(bf16)
                for a in range(3):
                    i = p - a
                    if 0 <= i < block_rows:
                        for b, piece in enumerate((left, mid, right)):
                            taken[
                                s % 2,
                                pl.ds((3 * a + b) * channels + j * chan_local, chan_local),
                                pl.ds(i * block_cols, block_cols),
                            ] = piece
        conv = ein(conv_ref[...], taken[s % 2], ((1,), (0,))) + bias
        squares = jnp.sum(conv * conv, axis=0, keepdims=True)
        normed = (conv * lax.rsqrt(squares / channels + norm_eps) * gain).astype(bf16)
        step = min(hidden, 256)
        for h in range(0, hidden, step):
            pre = ein(in_ref[pl.ds(h, step), :], normed, ((1,), (0,)))
            pre = pre + hid_col_ref[pl.ds(h, step), 2:3]
            act = pre * (0.5 * lax.erf(pre * (0.5**0.5)) + 0.5)
            hid[s % 2, pl.ds(h, step), :] = act.astype(bf16)
        upd = ein(out_ref[...], hid[s % 2], ((1,), (0,))).astype(bf16)
        for j in range(groups):
            for i in range(block_rows):
                upd_ref[j, s, i] = upd[
                    j * chan_local : (j + 1) * chan_local, i * block_cols : (i + 1) * block_cols
                ]


def block_step(body, rims, weights):
    groups, per, block_rows, chan_local, block_cols = body.shape
    channels = groups * chan_local
    hidden = weights[1].shape[0]
    cells = per * block_rows * block_cols
    return pl.pallas_call(
        block_kernel,
        out_shape=shape(body.shape),
        in_specs=[VMEM] * 7,
        out_specs=VMEM,
        scratch_shapes=[
            pltpu.VMEM((2, 9 * channels, block_rows * block_cols), bf16),
            pltpu.VMEM((2, hidden, block_rows * block_cols), bf16),
        ],
        compiler_params=params(),
        cost_estimate=pl.CostEstimate(
            flops=2 * cells * (9 * channels * channels + 2 * channels * hidden),
            bytes_accessed=8 * 1024 * 1024,
            transcendentals=0,
        ),
        name="block_step",
    )(body, rims, *weights)


def forcing_kernel(row_ref, side_ref, table_ref, out_ref, wide, got):
    slot_count, block_rows, chan_local, block_cols = out_ref.shape
    lanes = table_ref.shape[1]
    wide[...] = table_ref[...].astype(f32)

    def one(q, _):
        for k in range(block_cols):
            got[pl.ds(k, 1), :] = wide[pl.ds(row_ref[q, k], 1), :]
        across = got[...].T
        side = side_ref[pl.ds(q, 1), :]
        total = across[:chan_local]
        for k in range(1, lanes // chan_local):
            total = jnp.where(side == k, across[k * chan_local : (k + 1) * chan_local], total)
        out_ref[q // block_rows, q % block_rows] = total.astype(bf16)
        return 0

    lax.fori_loop(0, slot_count * block_rows, one, 0)


def forcing_of(table, remap, rows_local, chan_local):
    slot_count, block_rows, block_cols = remap.shape
    side_by = 128 // chan_local
    part = rows_local // side_by
    target = jnp.clip(remap, 0, table.shape[0] * side_by - 1).reshape(-1, block_cols)
    tile_of = target // rows_local
    within = target - tile_of * rows_local
    side = within // part
    row = tile_of * part + within - side * part
    return pl.pallas_call(
        forcing_kernel,
        out_shape=shape((slot_count, block_rows, chan_local, block_cols)),
        in_specs=[SMEM, VMEM, VMEM],
        out_specs=VMEM,
        scratch_shapes=[
            pltpu.VMEM(table.shape, f32),
            pltpu.VMEM((block_cols, table.shape[1]), f32),
        ],
        compiler_params=params(),
        cost_estimate=pl.CostEstimate(
            flops=0, bytes_accessed=32 * 1024 * 1024, transcendentals=0
        ),
        name="forcing",
    )(row, side, table)


def final_kernel(xt_ref, upd_ref, forcing_ref, mask_ref, scale_ref, out_ref):
    slot_count, block_rows, chan_local, block_cols = xt_ref.shape
    scale = scale_ref[...].astype(f32)
    for s in range(slot_count):
        total = xt_ref[s].astype(f32) + scale[None] * upd_ref[s].astype(f32)
        total = total + forcing_ref[s].astype(f32)
        total = mask_ref[s].astype(f32)[:, None, :] * total
        out_ref[:, s] = jnp.swapaxes(total, 0, 1).astype(bf16)


def final_step(xt, update, forcing, cell_mask, layer_scale):
    slot_count, block_rows, chan_local, block_cols = xt.shape
    return pl.pallas_call(
        final_kernel,
        out_shape=shape((chan_local, slot_count, block_rows, block_cols)),
        in_specs=[VMEM] * 5,
        out_specs=VMEM,
        compiler_params=params(),
        name="final_step",
    )(xt, update, forcing, cell_mask, layer_scale[:, None])


def on_device(
    ocean_state,
    atmos,
    flux_weight,
    conv_weight,
    conv_bias,
    norm_gain,
    in_weight,
    in_bias,
    out_weight,
    layer_scale,
    cell_mask,
    neighbours,
    remap,
):
    chan_local, slot_count, block_rows, block_cols = ocean_state.shape
    groups = lax.axis_size(GROUP)
    tile_count = lax.axis_size("tile")
    per = slot_count // groups
    hid_local = in_weight.shape[1]

    xt, strips = prep(ocean_state)
    up = [(i, i + 1) for i in range(tile_count - 1)]
    strips_prev = lax.ppermute(strips, "tile", up)
    strips_next = lax.ppermute(strips, "tile", [(b, a) for a, b in up])
    body = lax.all_to_all(
        xt.reshape(groups, per, block_rows, chan_local, block_cols), GROUP, 0, 0, tiled=True
    )
    packed = pack_weights(conv_weight, conv_bias, norm_gain, in_weight, in_bias, out_weight)
    gathered = lax.all_gather(packed, GROUP, axis=0)
    flux = fluxes_of(atmos, flux_weight)
    table = lax.all_gather(flux, "tile", axis=0, tiled=True)

    first_slot = (lax.axis_index("tile") - 1) * slot_count
    rims = rims_of(strips_prev, strips, strips_next, neighbours, first_slot, groups)
    rims = lax.all_to_all(rims, GROUP, 0, 0, tiled=True)
    weights = unpack_weights(gathered, chan_local, hid_local)
    update = block_step(body, rims, weights)
    update, table = lax.optimization_barrier((update, table))
    update = lax.all_to_all(update, GROUP, 0, 0, tiled=True)
    update = update.reshape(xt.shape)
    forcing = forcing_of(table, remap, atmos.shape[0], chan_local)
    return final_step(xt, update, forcing, cell_mask, layer_scale)


def solution(mesh):
    placed = (
        P(("chan", "sec"), ("ens", "tile"), None, None),
        P(("ens", "tile"), None),
        P(None, ("chan", "sec")),
        P(None, None, ("chan", "sec")),
        P(("chan", "sec")),
        P(("chan", "sec")),
        P(None, ("chan", "sec")),
        P(("chan", "sec")),
        P(("chan", "sec"), None),
        P(("chan", "sec")),
        P("tile", None, None),
        P("tile", None),
        P("tile", None, None),
    )
    return jax.shard_map(
        on_device,
        mesh=mesh,
        in_specs=placed,
        out_specs=P(("chan", "sec"), ("ens", "tile"), None, None),
        check_vma=False,
    )
```

time: 305 us -> 106 us (0.35)
  local copies, waits for them, and re-layouts: 140 us -> 11.5 us
  blocking collectives: 55.6 us -> 0 us
  matrix products: 35.6 us -> 0 us
  Pallas kernels: 0 us -> 32 us
  other arithmetic: 22.6 us -> 0.11 us
  waiting for transfers between devices: 17.9 us -> 30.3 us
    gather x4 -> x0, local copies, waits for them, and re-layouts: 52.5 us -> none  [the longest x2 32.9 us: on_device(): values = jnp.take(piece, jnp.clip(targets, 0, piece.shape[1] - 1), axis=1)]
    dot_general x15 -> x0, matrix products: 35.6 us -> none  [the longest x1 20.7 us: on_device(): jnp.einsum('csij,ch->hsij', normed, full_in, preferred_element_type=jnp.f...]
    unnamed x1 -> x0, blocking collectives: 35.2 us -> none
    pallas_call x0 -> x8, Pallas kernels: none -> 32 us  [the longest x1 13.9 us: forcing_of(): pl.pallas_call(forcing_kernel, out_shape=shape((slot_count, block_rows, c...]
    squeeze x8 -> x0, local copies, waits for them, and re-layouts: 26 us -> none  [the longest x1 7.9 us: strips_of(): state[:, :, :, -1]]
    all_gather x3 -> x0, blocking collectives: 20.4 us -> none  [the longest x1 7.95 us: on_device(): lax.all_gather(out_weight, ('chan', 'sec'), axis=0, tiled=True)]
    all_to_all x2 -> x3, waiting for transfers between devices: 0.01 us -> 16.9 us  [the longest x1 10.7 us: on_device(): lax.all_to_all(xt.reshape(groups, per, block_rows, chan_local, block_cols...]
    slice x8 -> x2, local copies, waits for them, and re-layouts: 13.4 us -> 0.17 us  [the longest x1 0.08 us: rims_of(): base[:, 6]]
  transfers between devices with their start and end apart: 6 -> 7, of which waited for: 2 -> 6; matrix products, arithmetic and copies ran while one was open for 51% -> 1% of each run, Pallas kernels for 0% -> 26%
where the time goes in v1:
time: 106 us; the launch traced here: 105 us
  Pallas kernels  32 us (30%)
  waiting for transfers between devices  30.3 us (29%)
  starting transfers between devices  17.8 us (17%)
  between operations  13.6 us (13%)
  local copies, waits for them, and re-layouts  11.5 us (11%)
    pallas_call x1, Pallas kernels, forcing_of(): pl.pallas_call(forcing_kernel, out_shape=shape((slot_count, block_rows, c...  13.9 us
    all_to_all x1, waiting for transfers between devices, on_device(): lax.all_to_all(xt.reshape(groups, per, block_rows, chan_local, block_cols...  10.7 us
    unnamed x36, local copies, waits for them, and re-layouts  9.44 us
    pallas_call x1, Pallas kernels, block_step(): pl.pallas_call(block_kernel, out_shape=shape(body.shape), in_specs=[VMEM]...  8.08 us
    all_to_all x1, waiting for transfers between devices, on_device(): rims = lax.all_to_all(rims, GROUP, 0, 0, tiled=True)  5.9 us
    ppermute x1, starting transfers between devices, on_device(): strips_prev = lax.ppermute(strips, 'tile', up)  5.76 us
    all_gather x1, waiting for transfers between devices, on_device(): table = lax.all_gather(flux, 'tile', axis=0, tiled=True)  5.19 us
    ppermute x1, waiting for transfers between devices, on_device(): strips_next = lax.ppermute(strips, 'tile', [(b, a) for a, b in up])  5.04 us
  transfers between devices with their start and end apart: 7, of which 6 were waited for; matrix products, arithmetic and copies ran while one was open for 1% of the time, Pallas kernels for 26%

profile of v1, /device:TPU:0, one launch (start us, length us, event | category | flops | bytes accessed | tf_op | source)
XLA Modules:
  0.0 105.3 jit_solution(767948296689096587)
XLA Ops:
  6.5 0.0 all-gather.6.cloned.1.call-start
  6.5 0.7 broadcast_in_dim.25.in_bias_ref
  7.3 1.0 copy-done.4
  8.3 0.9 copy-done.5
  9.2 0.9 copy-done.6
  10.1 0.7 copy-done.9
  10.7 0.7 copy-done.10
  11.4 0.9 pack_weights.1
  12.3 0.0 all-gather.6.cloned.1.call-update
  12.3 0.0 copy-done.2
  12.3 0.0 copy-start.1
  12.3 0.0 copy-start.7
  12.3 1.7 %prep_state.1 = (bf16[16,4,64,128]{3,2,1,0:T(8,128)(2,1)}, bf16[33,64,128]{2,1,0:T(8,128)(2,1)S(1)}) custom-call(bf16[64,16,4,128]{3,2,1,0:T(4,128)(2,1)S(1)} %copy-done.2), custom_call_target="tpu_custom_call" | custom-call | tf_op jit(solution)/shard_map/prep_state/pallas_call | solution.py:50
  14.0 5.8 %collective-permute-start = (bf16[33,64,128]{2,1,0:T(8,128)(2,1)S(1)}, bf16[33,64,128]{2,1,0:T(8,128)(2,1)}, u32[]{:S(2)}, u32[]{:S(2)}) collective-permute-start(bf16[33,64,128]{2,1,0:T(8,128)(2,1)S(1)} %get-tuple-element.15.own_ref), channel_id=1, source_target_pairs={{0,4},{4,8},{8,12},{1,5},{5,9},{9,13},{2,6},{6,10},{10,14},{3,7},{... | collective-permute-start | bytes 1622024 | tf_op jit(solution)/shard_map/ppermute | solution.py:394
  19.8 1.3 %collective-permute-start.1 = (bf16[33,64,128]{2,1,0:T(8,128)(2,1)S(1)}, bf16[33,64,128]{2,1,0:T(8,128)(2,1)}, u32[]{:S(2)}, u32[]{:S(2)}) collective-permute-start(bf16[33,64,128]{2,1,0:T(8,128)(2,1)S(1)} %get-tuple-element.15.own_ref), channel_id=1, source_target_pairs={{4,0},{8,4},{12,8},{5,1},{9,5},{13,9},{6,2},{10,6},{14,10},{7,3},{... | collective-permute-start | bytes 1622024 | tf_op jit(solution)/shard_map/ppermute | solution.py:395
  21.1 3.5 %all-to-all-start = ((bf16[4,4,4,64,128]{4,3,2,1,0:T(8,128)(2,1)}), bf16[4,4,4,64,128]{4,3,2,1,0:T(8,128)(2,1)S(1)}, u32[]{:S(2)}, u32[]{:S(2)}) async-start(bf16[4,4,4,64,128]{4,3,2,1,0:T(8,128)(2,1)} %bitcast), calls=%async_computation | async-start | bytes 2097152 | tf_op jit(solution)/shard_map/all_to_all | solution.py:396
  24.6 0.0 copy-start.16
  24.7 0.0 all-gather.4.cloned.1.call-start
  24.7 0.0 copy-done.1
  24.7 0.0 copy-done.7
  24.7 1.3 %fluxes.1 = bf16[1024,128]{1,0:T(8,128)(2,1)} custom-call(bf16[2048,384]{1,0:T(8,128)(2,1)S(1)} %copy-done.1, bf16[64,384]{1,0:T(8,128)(2,1)S(1)} %bitcast.16), custom_call_target="tpu_custom_call" | custom-call | tf_op jit(solution)/shard_map/fluxes/pallas_call | solution.py:158
  26.0 0.0 all-gather.4.cloned.1.call-update
  26.0 0.0 copy-done.16
  26.1 0.1 copy.14
  26.2 0.1 copy.15
  26.3 0.1 copy.16
  26.4 0.1 copy.17
  26.4 0.1 copy.18
  26.5 0.1 copy.19
  26.6 0.1 copy.20
  26.7 0.1 copy.21
  26.8 0.1 copy.22
  26.9 0.1 copy.23
  26.9 0.1 copy.24
  27.0 0.1 copy.25
  27.1 0.1 stack.5
  27.2 0.1 reshape.56
  27.3 3.2 %collective-permute-done.prev_ref = bf16[33,64,128]{2,1,0:T(8,128)(2,1)} collective-permute-done((bf16[33,64,128]{2,1,0:T(8,128)(2,1)S(1)}, bf16[33,64,128]{2,1,0:T(8,128)(2,1)}, u32[]{:S(2)}, u32[]{:S(2)}) %collective-permute-start) | collective-permute-done | bytes 540704 | tf_op jit(solution)/shard_map/ppermute | solution.py:394
  30.5 5.0 %collective-permute-done.1.next_ref = bf16[33,64,128]{2,1,0:T(8,128)(2,1)} collective-permute-done((bf16[33,64,128]{2,1,0:T(8,128)(2,1)S(1)}, bf16[33,64,128]{2,1,0:T(8,128)(2,1)}, u32[]{:S(2)}, u32[]{:S(2)}) %collective-permute-start.1) | collective-permute-done | bytes 540704 | tf_op jit(solution)/shard_map/ppermute | solution.py:395
  35.5 2.3 %rims.1 = bf16[4,9,64,128]{3,2,1,0:T(8,128)(2,1)} custom-call(s32[2,16]{1,0:T(2,128)S(1)} %pad_add_fusion.entry_ref, s32[4,128]{1,0:T(4,128)S(1)} %pad.4.at_ref, bf16[33,64,128]{2,1,0:T(8,128)(2,1)} %collective-permute-done.prev_ref, bf16[33,64,128]{2,1,0:T(8,128)(2,1)S(1)} %get-tuple-element.15.own_ref, bf16[33,64,128]{2,1,0:T(8,128)(2,1)} %collective-permute-done.1.next_ref), custom_call_target="tpu_custom_call" | custom-call | tf_op jit(solution)/shard_map/rims/pallas_call | solution.py:212
  37.9 10.7 %all-to-all-done.body_ref = bf16[4,4,4,64,128]{4,3,2,1,0:T(8,128)(2,1)S(1)} async-done(((bf16[4,4,4,64,128]{4,3,2,1,0:T(8,128)(2,1)}), bf16[4,4,4,64,128]{4,3,2,1,0:T(8,128)(2,1)S(1)}, u32[]{:S(2)}, u32[]{:S(2)}) %all-to-all-start) | async-done | bytes 1048608 | tf_op jit(solution)/shard_map/all_to_all | solution.py:396
  48.6 3.5 %all-to-all-start.1 = ((bf16[4,9,64,128]{3,2,1,0:T(8,128)(2,1)}), bf16[4,9,64,128]{3,2,1,0:T(8,128)(2,1)S(1)}, u32[]{:S(2)}, u32[]{:S(2)}) async-start(bf16[4,9,64,128]{3,2,1,0:T(8,128)(2,1)} %rims.1), calls=%async_computation.1 | async-start | bytes 1179648 | tf_op jit(solution)/shard_map/all_to_all | solution.py:406
  52.1 0.0 all-gather.6.cloned.1.call-done
  52.1 0.0 copy-start
  52.1 1.6 %copy-done = bf16[4480,256]{1,0:T(8,128)(2,1)S(1)} copy-done((bf16[4480,256]{1,0:T(8,128)(2,1)S(1)}, bf16[4480,256]{1,0:T(8,128)(2,1)}, u32[]{:S(2)}) %copy-start) | copy-done | bytes 2293784
  53.7 0.3 unpack_weights.1
  54.1 0.0 copy-start.11
  54.1 0.8 copy-done.11
  54.9 0.8 copy-done.13
  55.7 5.9 %all-to-all-done.1.rim_ref = bf16[4,9,64,128]{3,2,1,0:T(8,128)(2,1)S(1)} async-done(((bf16[4,9,64,128]{3,2,1,0:T(8,128)(2,1)}), bf16[4,9,64,128]{3,2,1,0:T(8,128)(2,1)S(1)}, u32[]{:S(2)}, u32[]{:S(2)}) %all-to-all-start.1) | async-done | bytes 589856 | tf_op jit(solution)/shard_map/all_to_all | solution.py:406
  61.6 1.0 copy-done.12
  62.6 1.0 copy-done.14
  63.6 8.1 %block_step.1 = bf16[4,4,4,64,128]{4,3,2,1,0:T(8,128)(2,1)} custom-call(bf16[4,4,4,64,128]{4,3,2,1,0:T(8,128)(2,1)S(1)} %all-to-all-done.body_ref, bf16[4,9,64,128]{3,2,1,0:T(8,128)(2,1)S(1)} %all-to-all-done.1.rim_ref, bf16[256,2304]{1,0:T(8,128)(2,1)S(1)} %get-tuple-element.16.conv_ref, bf16[1024,256]{1,0:T(8,128)(2,1)S(1)} %get-tuple-element.17.in_ref, ...), custom_call_target="tpu_custom_call" | custom-call | flops 4563402752 | bytes 8388608 | tf_op jit(solution)/shard_map/block_step/pallas_call | solution.py:285
  71.7 5.2 %all-gather.4.cloned.1.call-done.table_ref = bf16[4096,128]{1,0:T(8,128)(2,1)} async-done(((bf16[1024,128]{1,0:T(8,128)(2,1)}), bf16[4096,128]{1,0:T(8,128)(2,1)}) %all-gather.4.cloned.1.call-update) | async-done | bytes 1048592 | tf_op jit(solution)/shard_map/all_gather | solution.py:402
  76.9 3.6 %all-to-all-start.2 = ((bf16[4,4,4,64,128]{4,3,2,1,0:T(8,128)(2,1)}), bf16[4,4,4,64,128]{4,3,2,1,0:T(8,128)(2,1)S(1)}, u32[]{:S(2)}, u32[]{:S(2)}) async-start(bf16[4,4,4,64,128]{4,3,2,1,0:T(8,128)(2,1)} %block_step.1), calls=%async_computation.2 | async-start | bytes 2097152 | tf_op jit(solution)/shard_map/all_to_all | solution.py:410
  80.6 0.0 copy-start.8
  80.6 0.0 copy-done.17
  80.6 0.1 copy.26.scale_ref
  80.7 0.0 copy-done.15
  80.7 0.1 multiply_subtract_fusion
  80.8 0.0 copy-done.3
  80.8 13.9 %forcing.1.forcing_ref = bf16[16,4,64,128]{3,2,1,0:T(8,128)(2,1)S(1)} custom-call(s32[64,128]{1,0:T(8,128)S(1)} %get-tuple-element.23.row_ref, s32[64,128]{1,0:T(8,128)S(1)} %get-tuple-element.24.side_ref, bf16[4096,128]{1,0:T(8,128)(2,1)S(1)} %copy-done.3), custom_call_target="tpu_custom_call" | custom-call | bytes 33554432 | tf_op jit(solution)/shard_map/forcing/pallas_call | solution.py:332
  94.7 0.3 all-to-all-done.2
  95.0 3.5 %final_step.1 = bf16[64,16,4,128]{3,2,1,0:T(4,128)(2,1)} custom-call(bf16[16,4,64,128]{3,2,1,0:T(8,128)(2,1)} %get-tuple-element.14.xt_ref, bf16[16,4,64,128]{3,2,1,0:T(8,128)(2,1)S(1)} %bitcast.13, bf16[16,4,64,128]{3,2,1,0:T(8,128)(2,1)S(1)} %forcing.1.forcing_ref, s32[16,4,128]{2,1,0:T(4,128)S(1)} %copy-done.8, bf16[64,1]{1,0:T(8,128)(2,1)S(1)} %copy.26.scale_ref), custom_call_target="tpu_custom_call" | custom-call | tf_op jit(solution)/shard_map/final_step/pallas_call | solution.py:361
  (20 shorter events, 0.1 us)
Async XLA Ops:
  6.5 5.8 %copy-start.2 = (bf16[64,16,4,128]{3,2,1,0:T(4,128)(2,1)S(1)}, bf16[64,16,4,128]{3,2,1,0:T(4,128)(2,1)}, u32[]{:S(2)}) copy-start(bf16[64,16,4,128]{3,2,1,0:T(4,128)(2,1)} %state_ref.1) | copy-start | bytes 3145732
  6.5 45.5 %all-gather.6.cloned.1.call-start = ((), (), s32[]{:S(2)}) async-start(), calls=%async_computation.4 | async-start | bytes 2867200 | tf_op jit(solution)/shard_map/all_gather | solution.py:400
  7.3 1.0 copy-start.4
  8.2 0.9 copy-start.5
  9.2 0.9 copy-start.6
  10.1 0.7 copy-start.9
  10.7 0.7 copy-start.10
  12.3 12.4 %copy-start.1 = (bf16[2048,384]{1,0:T(8,128)(2,1)S(1)}, bf16[2048,384]{1,0:T(8,128)(2,1)}, u32[]{:S(2)}) copy-start(bf16[2048,384]{1,0:T(8,128)(2,1)} %atmos_ref.1) | copy-start | bytes 4718596
  12.3 12.4 %copy-start.7 = (bf16[384,64]{0,1:T(8,128)(2,1)S(1)}, bf16[384,64]{0,1:T(8,128)(2,1)}, u32[]{:S(2)}) copy-start(bf16[384,64]{0,1:T(8,128)(2,1)} %param.15) | copy-start | bytes 147460
  14.0 16.4 %collective-permute-start = (bf16[33,64,128]{2,1,0:T(8,128)(2,1)S(1)}, bf16[33,64,128]{2,1,0:T(8,128)(2,1)}, u32[]{:S(2)}, u32[]{:S(2)}) collective-permute-start(bf16[33,64,128]{2,1,0:T(8,128)(2,1)S(1)} %get-tuple-element.15.own_ref), channel_id=1, source_target_pairs={{0,4},{4,8},{8,12},{1,5},{5,9},{9,13},{2,6},{6,10},{10,14},{3,7},{... | collective-permute-start | bytes 1622024 | tf_op jit(solution)/shard_map/ppermute | solution.py:394
  19.8 15.7 %collective-permute-start.1 = (bf16[33,64,128]{2,1,0:T(8,128)(2,1)S(1)}, bf16[33,64,128]{2,1,0:T(8,128)(2,1)}, u32[]{:S(2)}, u32[]{:S(2)}) collective-permute-start(bf16[33,64,128]{2,1,0:T(8,128)(2,1)S(1)} %get-tuple-element.15.own_ref), channel_id=1, source_target_pairs={{4,0},{8,4},{12,8},{5,1},{9,5},{13,9},{6,2},{10,6},{14,10},{7,3},{... | collective-permute-start | bytes 1622024 | tf_op jit(solution)/shard_map/ppermute | solution.py:395
  21.1 27.5 %all-to-all-start = ((bf16[4,4,4,64,128]{4,3,2,1,0:T(8,128)(2,1)}), bf16[4,4,4,64,128]{4,3,2,1,0:T(8,128)(2,1)S(1)}, u32[]{:S(2)}, u32[]{:S(2)}) async-start(bf16[4,4,4,64,128]{4,3,2,1,0:T(8,128)(2,1)} %bitcast), calls=%async_computation | async-start | bytes 2097152 | tf_op jit(solution)/shard_map/all_to_all | solution.py:396
  24.6 1.4 %copy-start.16 = (s32[16,8]{0,1:T(8,128)S(1)}, s32[16,8]{0,1:T(8,128)}, u32[]{:S(2)}) copy-start(s32[16,8]{0,1:T(8,128)} %param.24) | copy-start | bytes 1540
  24.7 52.3 %all-gather.4.cloned.1.call-start = ((), (), s32[]{:S(2)}) async-start(), calls=%async_computation.3 | async-start | bytes 1310720 | tf_op jit(solution)/shard_map/all_gather | solution.py:402
  48.6 13.0 %all-to-all-start.1 = ((bf16[4,9,64,128]{3,2,1,0:T(8,128)(2,1)}), bf16[4,9,64,128]{3,2,1,0:T(8,128)(2,1)S(1)}, u32[]{:S(2)}, u32[]{:S(2)}) async-start(bf16[4,9,64,128]{3,2,1,0:T(8,128)(2,1)} %rims.1), calls=%async_computation.1 | async-start | bytes 1179648 | tf_op jit(solution)/shard_map/all_to_all | solution.py:406
  52.1 1.6 %copy-start = (bf16[4480,256]{1,0:T(8,128)(2,1)S(1)}, bf16[4480,256]{1,0:T(8,128)(2,1)}, u32[]{:S(2)}) copy-start(bf16[4480,256]{1,0:T(8,128)(2,1)} %all-gather.6.cloned.1.call-done) | copy-start | bytes 6881284
  54.1 0.8 copy-start.11
  54.9 0.8 copy-start.13
  61.6 1.0 copy-start.12
  62.6 1.0 copy-start.14
  71.7 8.9 %copy-start.17 = (bf16[64]{0:T(256)(128)(2,1)S(1)}, bf16[64]{0:T(256)(128)(2,1)}, u32[]{:S(2)}) copy-start(bf16[64]{0:T(256)(128)(2,1)} %param.22) | copy-start | bytes 388
  71.7 9.0 %copy-start.15 = (s32[16,4,128]{2,1,0:T(4,128)S(1)}, s32[16,4,128]{2,1,0:T(4,128)}, u32[]{:S(2)}) copy-start(s32[16,4,128]{2,1,0:T(4,128)} %param.25) | copy-start | bytes 98308
  76.9 3.9 %copy-start.3 = (bf16[4096,128]{1,0:T(8,128)(2,1)S(1)}, bf16[4096,128]{1,0:T(8,128)(2,1)}, u32[]{:S(2)}) copy-start(bf16[4096,128]{1,0:T(8,128)(2,1)} %all-gather.4.cloned.1.call-done.table_ref) | copy-start | bytes 3145732
  76.9 18.1 %all-to-all-start.2 = ((bf16[4,4,4,64,128]{4,3,2,1,0:T(8,128)(2,1)}), bf16[4,4,4,64,128]{4,3,2,1,0:T(8,128)(2,1)S(1)}, u32[]{:S(2)}, u32[]{:S(2)}) async-start(bf16[4,4,4,64,128]{4,3,2,1,0:T(8,128)(2,1)} %block_step.1), calls=%async_computation.2 | async-start | bytes 2097152 | tf_op jit(solution)/shard_map/all_to_all | solution.py:410
  80.6 14.4 %copy-start.8 = (s32[16,4,128]{2,1,0:T(4,128)S(1)}, s32[16,4,128]{2,1,0:T(4,128)}, u32[]{:S(2)}) copy-start(s32[16,4,128]{2,1,0:T(4,128)} %mask_ref.1) | copy-start | bytes 98308
Sparse Core Ops, SparseCore 0:
  12.4 35.9 all-gather.5
  50.0 26.8 all-gather.3
